TPU v7x, 32 devices: a whole 2x2x4 slice. The times are simulated.
32 devices in a mesh: groups: 2 (over y), sector: 4 (over z), op: 4 (over x, core).
Axes of the slice: x: 2, y: 2, z: 4, core: 2. Of those that a mesh axis runs over, the one named last changes fastest.
Arguments:
- states: bfloat16 [4, 4, 4, 64, 128], P('groups', 'sector'), parts along dimension 0, may hold values from -6 to 6
- left_ops: bfloat16 [16, 8, 64, 64], P('op', ('groups', 'sector')), parts along dimension 1, may hold values from -3 to 3
- right_ops: bfloat16 [16, 8, 128, 128], P('op', ('groups', 'sector')), parts along dimension 1, may hold values from -3 to 3
- rows_live: int32 [8], P('groups'), parts along dimension 0, may hold values from 32 to 64
- cols_live: int32 [8], P('groups'), parts along dimension 0, may hold values from 64 to 128
- block_live: int32 [8, 4], P('groups'), parts along dimension 0, may hold values 0 or 1
Outputs:
- sigma_out: bfloat16 [4, 4, 4, 64, 128], P('groups', 'op', 'sector'), parts along dimension 0
- rayleigh: float32 [4, 2], P('groups'), parts along dimension 0
- correlation: float32 [4, 2], P('groups'), parts along dimension 0
There are 2 independent parts, one for each index of `groups`. A program takes and returns all parts, laid end to end along the dimension named above; each array names one. Nothing has to cross between parts.
All inputs are finite; a program needn't handle non-finite values.
Results may differ from a plain program's by a relative error of at most 0.0052.
Values may be sent and summed in bfloat16 or wider, within the bound.
A program may use at most 64 MiB of HBM per device.

v0:
```python
import jax
import jax.numpy as jnp
from jax import lax
from jax.sharding import PartitionSpec as P


def on_device(states, left_ops, right_ops, rows_live, cols_live, block_live):
    sectors = states.shape[1]
    left_rows = left_ops.shape[2]
    right_cols = right_ops.shape[2]
    row_ok = jnp.arange(left_rows)[None, :] < rows_live[:, None]
    col_ok = jnp.arange(right_cols)[None, :] < cols_live[:, None]
    first_own = lax.axis_index("sector") * sectors
    own_blocks = lax.dynamic_slice_in_dim(block_live, first_own, sectors, 0)
    own_rows = lax.dynamic_slice_in_dim(row_ok, first_own, sectors, 0)
    live_left = (
        (own_blocks[:, :, None, None] == 1) & own_rows[:, None, :, None] & col_ok[None, :, None, :]
    )
    masked = jnp.where(live_left[None], states, jnp.zeros_like(states))
    share_rows = block_live.shape[0] // lax.axis_size("op")
    first_share = lax.axis_index("op") * share_rows
    left_done = jnp.einsum(
        "kaxy,vabyz->kvabxz", left_ops, masked, preferred_element_type=jnp.float32
    ).astype(jnp.bfloat16)
    moved_terms, states_moved = (
        lax.all_to_all(left_done, "sector", split_axis=3, concat_axis=2, tiled=True),
        lax.all_to_all(masked[None], "sector", split_axis=3, concat_axis=2, tiled=True),
    )
    states_right = states_moved[0]
    partial_value = jnp.einsum(
        "kvabxy,kbzy->vabxz", moved_terms, right_ops, preferred_element_type=jnp.float32
    )
    summed = lax.psum(partial_value, "op")
    summed = lax.dynamic_slice_in_dim(summed, first_share, share_rows, 1)
    local_short = lax.dynamic_slice_in_dim(states_right, first_share, share_rows, 1)
    part_blocks = lax.dynamic_slice(block_live, (first_share, first_own), (share_rows, sectors))
    part_rows = lax.dynamic_slice_in_dim(row_ok, first_share, share_rows, 0)
    part_cols = lax.dynamic_slice_in_dim(col_ok, first_own, sectors, 0)
    live_right = (
        (part_blocks[:, :, None, None] == 1)
        & part_rows[:, None, :, None]
        & part_cols[None, :, None, :]
    )
    summed = jnp.where(live_right[None], summed, jnp.float32(0.0))
    sigma_out = summed.astype(jnp.bfloat16)
    local_states = local_short.astype(jnp.float32)
    ray_local = jnp.einsum("vabxy,wabxy->vw", local_states, summed, precision=lax.Precision.HIGHEST)
    norm_scale = jnp.float32(
        1.0 / (block_live.shape[0] * block_live.shape[1] * left_rows * right_cols)
    )
    own_correlation = jnp.einsum(
        "vabxy,wabxy->vw", masked, masked, preferred_element_type=jnp.float32
    )
    correlation = lax.psum(own_correlation, "sector")
    rayleigh = lax.psum(ray_local, ("sector", "op"))
    return (sigma_out, rayleigh * norm_scale, correlation * norm_scale)


def solution(mesh):
    placed = (
        P("groups", "sector", None, None, None),
        P("op", ("groups", "sector"), None, None),
        P("op", ("groups", "sector"), None, None),
        P("groups"),
        P("groups"),
        P("groups", None),
    )
    return jax.shard_map(
        on_device,
        mesh=mesh,
        in_specs=placed,
        out_specs=(P("groups", "op", "sector", None, None), P("groups", None), P("groups", None)),
        check_vma=False,
    )
```

profile of v0, /device:TPU:0, one launch (start us, length us, event | category | flops | bytes accessed | tf_op | source)
XLA Modules:
  0.0 115.8 jit_solution(5424414282004523827)
XLA Ops:
  7.2 0.7 copy-done.2
  7.9 0.6 dynamic_slice.21
  8.6 0.1 iota_compare_fusion
  8.6 0.6 copy-done.4
  9.2 0.1 iota_compare_fusion.1
  10.0 0.1 broadcast_and_fusion.2
  10.0 0.1 broadcast_and_fusion
  10.2 1.6 %fusion.12 = (bf16[2,4,64,128]{3,2,0,1:T(8,128)(2,1)S(1)}, bf16[1,2,1,4,64,128]{5,4,1,2,0,3:T(8,128)(2,1)}, bf16[2,4,64,128,1]{3,2,0,1,4:T(8,128)(2,1)S(1)}) fusion(bf16[2,1,4,64,128]{4,3,2,1,0:T(8,128)(2,1)} %param.6, pred[4,64,128]{2,1,0:T(8,128)(4,1)S(1)} %broadcast_and_fusion), kind=kLoop, calls=%fused_computation.19 | loop fusion | flops 65536 | bytes 557056 | tf_op jit(solution)/shard_map/reshape.12
  11.8 0.3 fusion
  12.1 0.8 copy.16
  12.9 6.3 %all-to-all-start = ((bf16[4,2,1,4,64,128]{5,4,0,1,2,3:T(8,128)(2,1)}), bf16[4,2,1,4,64,128]{5,4,0,1,2,3:T(8,128)(2,1)S(1)}, u32[]{:S(2)}, u32[]{:S(2)}) async-start(bf16[4,2,1,4,64,128]{5,4,0,1,2,3:T(8,128)(2,1)} %copy.16), calls=%async_computation | async-start | bytes 1048576 | tf_op jit(solution)/shard_map/all_to_all | solution.py:26
  19.2 0.5 convolution_bitcast_fusion.1
  19.7 14.0 %all-to-all-done = bf16[4,2,1,4,64,128]{5,4,0,1,2,3:T(8,128)(2,1)S(1)} async-done(((bf16[4,2,1,4,64,128]{5,4,0,1,2,3:T(8,128)(2,1)}), bf16[4,2,1,4,64,128]{5,4,0,1,2,3:T(8,128)(2,1)S(1)}, u32[]{:S(2)}, u32[]{:S(2)}) %all-to-all-start) | async-done | bytes 524320 | tf_op jit(solution)/shard_map/all_to_all | solution.py:26
  33.7 3.3 %all-to-all-start.1 = ((bf16[1,2,1,4,64,128]{5,4,1,2,0,3:T(8,128)(2,1)}), bf16[1,2,1,4,64,128]{5,4,1,2,0,3:T(8,128)(2,1)S(1)}, u32[]{:S(2)}, u32[]{:S(2)}) async-start(bf16[1,2,1,4,64,128]{5,4,1,2,0,3:T(8,128)(2,1)} %get-tuple-element.10), calls=%async_computation.1 | async-start | bytes 262144 | tf_op jit(solution)/shard_map/all_to_all | solution.py:27
  37.1 1.0 convolution_bitcast_fusion
  38.1 0.1 broadcast_and_fusion.1
  38.2 12.1 %psum.23 = f32[2,2]{1,0:T(2,128)S(1)} all-reduce(f32[2,2]{1,0:T(2,128)S(1)} %convolution_bitcast_fusion.1), channel_id=1, replica_groups=mesh['groups'=2,'sector'=4,'op'=4] {'sector'}, use_global_device_ids=true, to_apply=%region_2.3 | all-reduce | flops 4 | bytes 32 | tf_op jit(solution)/shard_map/psum | solution.py:54
  50.3 23.4 %all-reduce.2.cloned.1.call-done = f32[2,4,1,64,128]{4,3,1,0,2:T(8,128)} async-done(((f32[2,4,1,64,128]{4,3,1,0,2:T(8,128)}), f32[2,4,1,64,128]{4,3,1,0,2:T(8,128)}) %all-reduce.2.cloned.1.call-update) | async-done | bytes 262160 | tf_op jit(solution)/shard_map/psum | solution.py:33
  73.6 0.8 fusion.8
  74.5 0.4 convolution_bitcast_fusion.2
  74.9 0.6 broadcast_multiply_fusion
  75.5 31.4 %psum.22 = f32[2,2]{1,0:T(2,128)S(1)} all-reduce(f32[2,2]{1,0:T(2,128)S(1)} %convolution_bitcast_fusion.2), channel_id=1, replica_groups=mesh['groups'=2,'sector'=4,'op'=4] {'sector','op'}, use_global_device_ids=true, to_apply=%region_1.2 | all-reduce | flops 4 | bytes 32 | tf_op jit(solution)/shard_map/psum | solution.py:55
  106.9 0.6 broadcast_multiply_fusion.1
  107.4 1.5 %fusion.13 = bf16[2,1,1,64,128]{4,3,2,1,0:T(8,128)(2,1)} fusion(f32[2,4,1,64,128]{4,3,1,0,2:T(8,128)} %all-reduce.2.cloned.1.call-done, s32[]{:T(128)S(6)} %select_n.20, pred[64,128]{1,0:T(8,128)(4,1)S(1)} %broadcast_and_fusion.1), kind=kLoop, calls=%fused_computation.20 | loop fusion | flops 16384 | bytes 73732
  (15 shorter events, 0.2 us)
Async XLA Ops:
  7.2 29.9 %copy-start = (bf16[4,1,128,128]{3,2,1,0:T(8,128)(2,1)S(1)}, bf16[4,1,128,128]{3,2,1,0:T(8,128)(2,1)}, u32[]{:S(2)}) copy-start(bf16[4,1,128,128]{3,2,1,0:T(8,128)(2,1)} %param.8) | copy-start | bytes 393220
  7.2 0.7 copy-start.2
  7.9 0.7 copy-start.3
  8.6 0.7 copy-start.4
  10.2 1.6 %copy-start.1 = (bf16[4,1,64,64]{3,2,1,0:T(8,128)(2,1)S(1)}, bf16[4,1,64,64]{3,2,1,0:T(8,128)(2,1)}, u32[]{:S(2)}) copy-start(bf16[4,1,64,64]{3,2,1,0:T(8,128)(2,1)} %param.7) | copy-start | bytes 98308
  12.9 20.8 %all-to-all-start = ((bf16[4,2,1,4,64,128]{5,4,0,1,2,3:T(8,128)(2,1)}), bf16[4,2,1,4,64,128]{5,4,0,1,2,3:T(8,128)(2,1)S(1)}, u32[]{:S(2)}, u32[]{:S(2)}) async-start(bf16[4,2,1,4,64,128]{5,4,0,1,2,3:T(8,128)(2,1)} %copy.16), calls=%async_computation | async-start | bytes 1048576 | tf_op jit(solution)/shard_map/all_to_all | solution.py:26
  33.7 16.6 %all-to-all-start.1 = ((bf16[1,2,1,4,64,128]{5,4,1,2,0,3:T(8,128)(2,1)}), bf16[1,2,1,4,64,128]{5,4,1,2,0,3:T(8,128)(2,1)S(1)}, u32[]{:S(2)}, u32[]{:S(2)}) async-start(bf16[1,2,1,4,64,128]{5,4,1,2,0,3:T(8,128)(2,1)} %get-tuple-element.10), calls=%async_computation.1 | async-start | bytes 262144 | tf_op jit(solution)/shard_map/all_to_all | solution.py:27
  37.0 36.6 %all-reduce.2.cloned.1.call-start = ((), (), s32[]{:S(2)}) async-start(), calls=%async_computation.2 | async-start | bytes 524288 | tf_op jit(solution)/shard_map/psum | solution.py:33
Sparse Core Ops, SparseCore 0:
  40.2 33.3 all-reduce.1
where the time goes:
time: 116 us
  blocking collectives  43.5 us (38%)
  waiting for transfers between devices  37.3 us (32%)
  between operations  14.8 us (13%)
  starting transfers between devices  9.69 us (8%)
  other arithmetic  5.49 us (5%)
  local copies, waits for them, and re-layouts  2.8 us (2%)
  matrix products  2.19 us (2%)
    psum x1, blocking collectives, on_device(): rayleigh = lax.psum(ray_local, ('sector', 'op'))  31.4 us
    psum x1, waiting for transfers between devices, on_device(): summed = lax.psum(partial_value, 'op')  23.4 us
    all_to_all x1, waiting for transfers between devices, on_device(): lax.all_to_all(left_done, 'sector', split_axis=3, concat_axis=2, tiled=True)  14 us
    psum x1, blocking collectives, on_device(): correlation = lax.psum(own_correlation, 'sector')  12.1 us
    all_to_all x1, starting transfers between devices, on_device(): lax.all_to_all(left_done, 'sector', split_axis=3, concat_axis=2, tiled=True)  6.32 us
    all_to_all x1, starting transfers between devices, on_device(): lax.all_to_all(masked[None], 'sector', split_axis=3, concat_axis=2, tiled...  3.32 us
    another operation x2, other arithmetic  2.46 us
  transfers between devices with their start and end apart: 3, of which 2 were waited for; matrix products, arithmetic and copies ran while one was open for 1% of the time, Pallas kernels for 0%

commit v1 on v0

v1 whole, which is shorter than its diff:
```python
import functools

import jax
import jax.numpy as jnp
from jax import lax
from jax.experimental import pallas as pl
from jax.experimental.pallas import tpu as pltpu
from jax.sharding import PartitionSpec as P

MESH = pl.DeviceIdType.MESH


def each(count, body):
    if count <= 16:
        for i in range(count):
            body(i)
    else:
        lax.fori_loop(0, count, lambda i, c: (body(i), c)[1], 0)


def kernel(
    n, ops, norm,
    rows_ref, cols_ref, blocks_ref, states_ref, left_ref, right_ref,
    sigma_ref, ray_ref, corr_ref,
    left_own, left_send_buf, left_all, right_all, states_all, stats,
    local_sem, left_ss, left_rs, right_ss, right_rs, st_ss, st_rs, stat_ss, stat_rs,
):
    s = lax.axis_index("sector")
    o = lax.axis_index("op")
    share = states_all.shape[0]
    kl = left_own.shape[0]
    rows, width = states_all.shape[2:]
    owner = s // share
    slot = lax.rem(s, share)
    mate = o + 1 - 2 * lax.rem(o, 2)

    load_left = pltpu.make_async_copy(left_ref.at[:, 0], left_own, local_sem.at[0])
    load_left.start()
    load_right = pltpu.make_async_copy(right_ref.at[:, 0], right_all.at[o], local_sem.at[1])
    load_right.start()
    load_states = pltpu.make_async_copy(
        states_ref.at[:, 0, s], states_all.at[slot], local_sem.at[2]
    )

    @pl.when(owner == o)
    def _():
        load_states.start()

    barrier = pltpu.get_barrier_semaphore()

    def greet(r):
        pl.semaphore_signal(
            barrier,
            inc=1,
            device_id={
                "sector": lax.rem(s + (r + 1) // ops, n),
                "op": lax.rem(o + lax.rem(r + 1, ops), ops),
            },
            device_id_type=MESH,
        )

    each(n * ops - 1, greet)

    load_left.wait()
    packed = [
        jnp.concatenate([left_own[2 * j], left_own[2 * j + 1]], axis=1) for j in range(kl // 2)
    ]
    for j in range(kl // 2):
        left_send_buf[j] = packed[j]

    @pl.when(owner == o)
    def _():
        for j in range(kl // 2):
            left_all[slot, o, j] = packed[j]

    pl.semaphore_wait(barrier, n * ops - 1)

    def right_copy(origin, src, to, sem):
        return pltpu.make_async_remote_copy(
            src_ref=src,
            dst_ref=right_all.at[origin],
            send_sem=right_ss.at[sem],
            recv_sem=right_rs.at[origin],
            device_id={"op": to},
            device_id_type=MESH,
        )

    far = [lax.rem(o + 2 * p, ops) for p in range(1, ops // 2)]
    own_right = right_ref.at[:, 0]
    sends = [right_copy(o, own_right, far[p], p) for p in range(len(far))]
    sends.append(right_copy(o, own_right, mate, len(far)))
    for copy in sends:
        copy.start()

    def left_copy(d):
        return pltpu.make_async_remote_copy(
            src_ref=left_send_buf,
            dst_ref=left_all.at[slot, o],
            send_sem=left_ss.at[d],
            recv_sem=left_rs.at[slot, o],
            device_id={"sector": lax.rem(s + d, n), "op": owner},
            device_id_type=MESH,
        )

    def state_copy(d):
        to = lax.rem(s + d, n)
        return pltpu.make_async_remote_copy(
            src_ref=states_ref.at[:, 0, to],
            dst_ref=states_all.at[slot],
            send_sem=st_ss.at[d],
            recv_sem=st_rs.at[slot],
            device_id={"sector": to, "op": o},
            device_id_type=MESH,
        )

    @pl.when(owner == o)
    def _():
        each(n - 1, lambda d: state_copy(d + 1).start())

    each(n - 1, lambda d: left_copy(d + 1).start())

    @pl.when(owner != o)
    def _():
        left_copy(0).start()

    for p in range(len(far)):
        origin = far[p]
        right_copy(origin, right_all.at[origin], mate, len(far) + 1 + p).wait_recv()
        copy = right_copy(origin, right_all.at[origin], mate, len(far) + 1 + p)
        copy.start()
        sends.append(copy)

    load_right.wait()

    @pl.when(owner == o)
    def _():
        load_states.wait()

    row_at = lax.broadcasted_iota(jnp.int32, (rows, width), 0)
    col_at = lax.broadcasted_iota(jnp.int32, (rows, width), 1)
    zero = jnp.zeros((rows, width), jnp.bfloat16)
    totals = [jnp.zeros((1, width), jnp.float32) for _ in range(8)]

    def one_block(i, totals, first):
        a = o * share + i

        @pl.when(a != s)
        def _():
            state_copy_in(i).wait_recv()

        live = (
            (row_at < rows_ref[a]) & (col_at < cols_ref[s]) & (blocks_ref[a, s] == 1)
        )
        masked = [
            jnp.where(live, states_all[i, v].astype(jnp.float32), 0.0) for v in range(2)
        ]
        narrow = [m.astype(jnp.bfloat16) for m in masked]
        pairs = [
            jnp.concatenate(
                [
                    jnp.concatenate([m, zero], axis=1),
                    jnp.concatenate([zero, m], axis=1),
                ],
                axis=0,
            )
            for m in narrow
        ]
        acc = jnp.zeros((2 * rows, width), jnp.float32)
        for step in range(ops):
            if step == 0:
                g = o
            elif step == 1:
                g = mate
            elif step % 2 == 0:
                g = far[step // 2 - 1]
            else:
                f = far[step // 2 - 1]
                g = f + 1 - 2 * lax.rem(f, 2)

            @pl.when(jnp.logical_or(a != s, g != o))
            def _():
                left_copy_in(i, g).wait_recv()

            if first and step % 2 == 1:
                right_copy(g, right_all.at[g], mate, 0).wait_recv()
            lhs = left_all[i, g].reshape(kl // 2 * rows, 2 * rows)
            done = []
            for v in range(2):
                t = jnp.dot(lhs, pairs[v], preferred_element_type=jnp.float32)
                t = t.astype(jnp.bfloat16)
                done.append(
                    jnp.concatenate(
                        [t[j * rows:(j + 1) * rows] for j in range(kl // 2)], axis=1
                    )
                )
            rhs = jnp.concatenate([right_all[g, k] for k in range(kl)], axis=1)
            acc += lax.dot_general(
                jnp.concatenate(done, axis=0), rhs, (((1,), (1,)), ((), ())),
                preferred_element_type=jnp.float32,
            )
        summed = [
            jnp.where(live, acc[v * rows:(v + 1) * rows], 0.0) for v in range(2)
        ]
        for v in range(2):
            sigma_ref[v, i, 0] = summed[v].astype(jnp.bfloat16)
        out = []
        for right in (summed, masked):
            for v in range(2):
                for w in range(2):
                    out.append(jnp.sum(masked[v] * right[w], axis=0, keepdims=True))
        return [x + y for x, y in zip(totals, out)]

    def state_copy_in(i):
        return pltpu.make_async_remote_copy(
            src_ref=states_ref.at[:, 0, s],
            dst_ref=states_all.at[i],
            send_sem=st_ss.at[0],
            recv_sem=st_rs.at[i],
            device_id={"sector": lax.rem(s + 1, n), "op": o},
            device_id_type=MESH,
        )

    def left_copy_in(i, g):
        return pltpu.make_async_remote_copy(
            src_ref=left_send_buf,
            dst_ref=left_all.at[i, g],
            send_sem=left_ss.at[0],
            recv_sem=left_rs.at[i, g],
            device_id={"sector": lax.rem(s + 1, n), "op": o},
            device_id_type=MESH,
        )

    totals = one_block(0, totals, True)
    if share > 1:
        totals = lax.fori_loop(
            1, share, lambda i, t: tuple(one_block(i, list(t), False)), tuple(totals)
        )

    rank = s * ops + o
    stats[rank] = jnp.concatenate(list(totals), axis=0)

    def tell(r):
        pltpu.make_async_remote_copy(
            src_ref=stats.at[rank],
            dst_ref=stats.at[rank],
            send_sem=stat_ss,
            recv_sem=stat_rs,
            device_id={
                "sector": lax.rem(s + (r + 1) // ops, n),
                "op": lax.rem(o + lax.rem(r + 1, ops), ops),
            },
            device_id_type=MESH,
        ).start()

    each(n * ops - 1, tell)

    for copy in sends:
        copy.wait_send()

    @pl.when(owner == o)
    def _():
        each(n - 1, lambda d: state_copy(d + 1).wait_send())

    each(n - 1, lambda d: left_copy(d + 1).wait_send())

    @pl.when(owner != o)
    def _():
        left_copy(0).wait_send()

    others = stats.at[pl.ds(0, n * ops - 1)]
    both = pltpu.make_async_remote_copy(
        src_ref=others, dst_ref=others, send_sem=stat_ss, recv_sem=stat_rs,
        device_id={"sector": lax.rem(s + 1, n), "op": o}, device_id_type=MESH,
    )
    both.wait_recv()
    both.wait_send()
    result = jnp.sum(jnp.sum(stats[...], axis=0), axis=1, keepdims=True) * norm
    for v in range(2):
        for w in range(2):
            at = 2 * v + w
            ray_ref[v:v + 1, w:w + 1] = result[at:at + 1]
            corr_ref[v:v + 1, w:w + 1] = result[4 + at:5 + at]


def on_device(mesh, states, left_ops, right_ops, rows_live, cols_live, block_live):
    n = mesh.shape["sector"]
    ops = mesh.shape["op"]
    kl, _, rows, _ = left_ops.shape
    width = right_ops.shape[2]
    nv = states.shape[0]
    left_sectors, right_sectors = block_live.shape
    share = left_sectors // ops
    assert nv == 2 and kl % 2 == 0 and ops % 2 == 0
    assert left_ops.shape[1] == 1 and right_ops.shape[1] == 1 and states.shape[1] == 1
    norm = 1.0 / (left_sectors * right_sectors * rows * width)
    smem = pl.BlockSpec(memory_space=pltpu.SMEM)
    vmem = pl.BlockSpec(memory_space=pltpu.VMEM)
    anywhere = pl.BlockSpec(memory_space=pl.ANY)
    dma = pltpu.SemaphoreType.DMA
    flops = 2 * nv * share * ops * kl * rows * width * (rows + width)
    return pl.pallas_call(
        functools.partial(kernel, n, ops, norm),
        out_shape=(
            jax.ShapeDtypeStruct((nv, share, 1, rows, width), jnp.bfloat16),
            jax.ShapeDtypeStruct((nv, nv), jnp.float32),
            jax.ShapeDtypeStruct((nv, nv), jnp.float32),
        ),
        in_specs=[smem, smem, smem, anywhere, anywhere, anywhere],
        out_specs=(vmem, vmem, vmem),
        scratch_shapes=[
            pltpu.VMEM((kl, rows, rows), jnp.bfloat16),
            pltpu.VMEM((kl // 2, rows, 2 * rows), jnp.bfloat16),
            pltpu.VMEM((share, ops, kl // 2, rows, 2 * rows), jnp.bfloat16),
            pltpu.VMEM((ops, kl, width, width), jnp.bfloat16),
            pltpu.VMEM((share, nv, rows, width), jnp.bfloat16),
            pltpu.VMEM((n * ops, 8, width), jnp.float32),
            dma((3,)),
            dma((n,)),
            dma((share, ops)),
            dma((ops,)),
            dma((ops,)),
            dma((n,)),
            dma((share,)),
            dma,
            dma,
        ],
        compiler_params=pltpu.CompilerParams(
            collective_id=0, has_side_effects=True, vmem_limit_bytes=48 * 1024 * 1024
        ),
        cost_estimate=pl.CostEstimate(
            flops=flops, bytes_accessed=1 << 20, transcendentals=0
        ),
    )(rows_live, cols_live, block_live, states, left_ops, right_ops)


def solution(mesh):
    placed = (
        P("groups", "sector", None, None, None),
        P("op", ("groups", "sector"), None, None),
        P("op", ("groups", "sector"), None, None),
        P("groups"),
        P("groups"),
        P("groups", None),
    )
    return jax.shard_map(
        functools.partial(on_device, mesh),
        mesh=mesh,
        in_specs=placed,
        out_specs=(P("groups", "op", "sector", None, None), P("groups", None), P("groups", None)),
        check_vma=False,
    )
```

time: 116 us -> 25.1 us (0.22)
  blocking collectives: 43.5 us -> 0 us
  waiting for transfers between devices: 37.3 us -> 0 us
  Pallas kernels: 0 us -> 17.8 us
  between operations: 14.8 us -> 0.65 us
  starting transfers between devices: 9.69 us -> 0 us
  other arithmetic: 5.49 us -> 0 us
  local copies, waits for them, and re-layouts: 2.8 us -> 6.37 us
  matrix products: 2.19 us -> 0 us
    psum x2 -> x0, blocking collectives: 43.5 us -> none  [the longest x1 31.4 us: on_device(): rayleigh = lax.psum(ray_local, ('sector', 'op'))]
    psum x1 -> x0, waiting for transfers between devices: 23.4 us -> none  [on_device(): summed = lax.psum(partial_value, 'op')]
    pallas_call x0 -> x1, Pallas kernels: none -> 17.8 us  [on_device(): pl.pallas_call(functools.partial(kernel, n, ops, norm), out_shape=(jax.Sh...]
    all_to_all x2 -> x0, waiting for transfers between devices: 14 us -> none  [the longest x1 14 us: on_device(): lax.all_to_all(left_done, 'sector', split_axis=3, concat_axis=2, tiled=True)]
    all_to_all x2 -> x0, starting transfers between devices: 9.65 us -> none  [the longest x1 6.32 us: on_device(): lax.all_to_all(left_done, 'sector', split_axis=3, concat_axis=2, tiled=True)]
    unnamed x10 -> x15, local copies, waits for them, and re-layouts: 1.37 us -> 6.37 us
    another operation x2 -> x0, other arithmetic: 2.46 us -> none
    dot_general x4 -> x0, matrix products: 2.19 us -> none  [the longest x1 0.99 us: on_device(): jnp.einsum('kvabxy,kbzy->vabxz', moved_terms, right_ops, preferred_elemen...]
  transfers between devices with their start and end apart: 3 -> 0, of which waited for: 2 -> 0; matrix products, arithmetic and copies ran while one was open for 1% -> 0% of each run, Pallas kernels for 0% -> 0%
where the time goes in v1:
time: 25.1 us; the launch traced here: 24.9 us
  Pallas kernels  17.8 us (71%)
  local copies, waits for them, and re-layouts  6.37 us (25%)
  between operations  0.65 us (3%)
    pallas_call x1, Pallas kernels, on_device(): pl.pallas_call(functools.partial(kernel, n, ops, norm), out_shape=(jax.Sh...  17.8 us
    unnamed x15, local copies, waits for them, and re-layouts  6.37 us

profile of v1, /device:TPU:0, one launch (start us, length us, event | category | flops | bytes accessed | tf_op | source)
XLA Modules:
  0.0 24.9 jit_solution(3897172695241577792)
XLA Ops:
  0.6 0.0 copy-start
  0.6 0.9 %copy-done = bf16[2,1,4,64,128]{4,3,2,1,0:T(8,128)(2,1)S(1)} copy-done((bf16[2,1,4,64,128]{4,3,2,1,0:T(8,128)(2,1)S(1)}, bf16[2,1,4,64,128]{4,3,2,1,0:T(8,128)(2,1)}, u32[]{:S(2)}) %copy-start) | copy-done | bytes 131096
  1.5 0.0 copy-start.1
  1.5 0.9 %copy-done.1 = bf16[4,1,128,128]{3,2,1,0:T(8,128)(2,1)S(1)} copy-done((bf16[4,1,128,128]{3,2,1,0:T(8,128)(2,1)S(1)}, bf16[4,1,128,128]{3,2,1,0:T(8,128)(2,1)}, u32[]{:S(2)}) %copy-start.1) | copy-done | bytes 131096
  2.4 0.0 copy-start.2
  2.4 0.8 %copy-done.2 = bf16[4,1,64,64]{3,2,1,0:T(8,128)(2,1)S(1)} copy-done((bf16[4,1,64,64]{3,2,1,0:T(8,128)(2,1)S(1)}, bf16[4,1,64,64]{3,2,1,0:T(8,128)(2,1)}, u32[]{:S(2)}) %copy-start.2) | copy-done | bytes 32792
  3.3 0.0 copy-start.3
  3.3 0.7 %copy-done.3 = s32[4,4]{1,0:T(4,128)S(1)} copy-done((s32[4,4]{1,0:T(4,128)S(1)}, s32[4,4]{1,0:T(4,128)}, u32[]{:S(2)}) %copy-start.3) | copy-done | bytes 88
  4.0 0.0 copy-start.4
  4.0 0.7 %copy-done.4 = s32[4]{0:T(128)S(1)} copy-done((s32[4]{0:T(128)S(1)}, s32[4]{0:T(128)}, u32[]{:S(2)}) %copy-start.4) | copy-done | bytes 40
  4.6 0.0 copy-start.5
  4.6 0.7 %copy-done.5 = s32[4]{0:T(128)S(1)} copy-done((s32[4]{0:T(128)S(1)}, s32[4]{0:T(128)}, u32[]{:S(2)}) %copy-start.5) | copy-done | bytes 40
  5.3 17.8 %shard_map.85 = (bf16[2,1,1,64,128]{4,3,2,1,0:T(8,128)(2,1)S(1)}, f32[2,2]{1,0:T(2,128)S(1)}, f32[2,2]{1,0:T(2,128)S(1)}) custom-call(s32[4]{0:T(128)S(1)} %copy-done.4, s32[4]{0:T(128)S(1)} %copy-done.5, s32[4,4]{1,0:T(4,128)S(1)} %copy-done.3, bf16[2,1,4,64,128]{4,3,2,1,0:T(8,128)(2,1)S(1)} %copy-done, bf16[4,1,64,64]{3,2,1,0:T(8,128)(2,1)S(1)} %copy-done.2, ...), custom_call_target="tpu_custom_call" | custom-call | flops 100663296 | bytes 1048576 | tf_op jit(solution)/shard_map/pallas_call | solution.py:301
  23.1 0.6 %copy.12 = bf16[2,1,1,64,128]{4,3,2,1,0:T(8,128)(2,1)} copy(bf16[2,1,1,64,128]{4,3,2,1,0:T(8,128)(2,1)S(1)} %get-tuple-element.6) | data formatting | bytes 65536
  23.7 0.6 %copy.13 = f32[2,2]{1,0:T(2,128)} copy(f32[2,2]{1,0:T(2,128)S(1)} %get-tuple-element.7) | data formatting | bytes 32
  24.3 0.6 %copy.14 = f32[2,2]{1,0:T(2,128)} copy(f32[2,2]{1,0:T(2,128)S(1)} %get-tuple-element.8) | data formatting | bytes 32
Async XLA Ops:
  0.6 0.9 %copy-start = (bf16[2,1,4,64,128]{4,3,2,1,0:T(8,128)(2,1)S(1)}, bf16[2,1,4,64,128]{4,3,2,1,0:T(8,128)(2,1)}, u32[]{:S(2)}) copy-start(bf16[2,1,4,64,128]{4,3,2,1,0:T(8,128)(2,1)} %states_ref.1) | copy-start | bytes 393220
  1.5 0.9 %copy-start.1 = (bf16[4,1,128,128]{3,2,1,0:T(8,128)(2,1)S(1)}, bf16[4,1,128,128]{3,2,1,0:T(8,128)(2,1)}, u32[]{:S(2)}) copy-start(bf16[4,1,128,128]{3,2,1,0:T(8,128)(2,1)} %right_ref.1) | copy-start | bytes 393220
  2.4 0.8 %copy-start.2 = (bf16[4,1,64,64]{3,2,1,0:T(8,128)(2,1)S(1)}, bf16[4,1,64,64]{3,2,1,0:T(8,128)(2,1)}, u32[]{:S(2)}) copy-start(bf16[4,1,64,64]{3,2,1,0:T(8,128)(2,1)} %left_ref.1) | copy-start | bytes 98308
  3.3 0.7 %copy-start.3 = (s32[4,4]{1,0:T(4,128)S(1)}, s32[4,4]{1,0:T(4,128)}, u32[]{:S(2)}) copy-start(s32[4,4]{1,0:T(4,128)} %blocks_ref.1) | copy-start | bytes 196
  4.0 0.7 %copy-start.4 = (s32[4]{0:T(128)S(1)}, s32[4]{0:T(128)}, u32[]{:S(2)}) copy-start(s32[4]{0:T(128)} %rows_ref.1) | copy-start | bytes 52
  4.6 0.7 %copy-start.5 = (s32[4]{0:T(128)S(1)}, s32[4]{0:T(128)}, u32[]{:S(2)}) copy-start(s32[4]{0:T(128)} %cols_ref.1) | copy-start | bytes 52

commit v2 on v1

--- a/solution.py
+++ b/solution.py
@@ -20,8 +20,10 @@
 
 def kernel(
     n, ops, norm,
-    rows_ref, cols_ref, blocks_ref, states_ref, left_ref, right_ref,
+    rows_hbm, cols_hbm, blocks_hbm, states_ref, left_ref, right_ref,
+    sigma_out, ray_out, corr_out,
     sigma_ref, ray_ref, corr_ref,
+    rows_ref, cols_ref, blocks_ref,
     left_own, left_send_buf, left_all, right_all, states_all, stats,
     local_sem, left_ss, left_rs, right_ss, right_rs, st_ss, st_rs, stat_ss, stat_rs,
 ):
@@ -46,6 +48,15 @@
     def _():
         load_states.start()
 
+    tables = [
+        pltpu.make_async_copy(src, dst, local_sem.at[3 + i])
+        for i, (src, dst) in enumerate(
+            [(rows_hbm, rows_ref), (cols_hbm, cols_ref), (blocks_hbm, blocks_ref)]
+        )
+    ]
+    for copy in tables:
+        copy.start()
+
     barrier = pltpu.get_barrier_semaphore()
 
     def greet(r):
@@ -131,6 +142,8 @@
         sends.append(copy)
 
     load_right.wait()
+    for copy in tables:
+        copy.wait()
 
     @pl.when(owner == o)
     def _():
@@ -236,6 +249,14 @@
             1, share, lambda i, t: tuple(one_block(i, list(t), False)), tuple(totals)
         )
 
+    outs = [
+        pltpu.make_async_copy(src, dst, local_sem.at[6 + i])
+        for i, (src, dst) in enumerate(
+            [(sigma_ref, sigma_out), (ray_ref, ray_out), (corr_ref, corr_out)]
+        )
+    ]
+    outs[0].start()
+
     rank = s * ops + o
     stats[rank] = jnp.concatenate(list(totals), axis=0)
 
@@ -280,6 +301,21 @@
             at = 2 * v + w
             ray_ref[v:v + 1, w:w + 1] = result[at:at + 1]
             corr_ref[v:v + 1, w:w + 1] = result[4 + at:5 + at]
+    for copy in outs[1:]:
+        copy.start()
+    for copy in outs:
+        copy.wait()
+
+
+def write_out(a, b, c, a_out, b_out, c_out, sem):
+    copies = [
+        pltpu.make_async_copy(src, dst, sem.at[i])
+        for i, (src, dst) in enumerate([(a, a_out), (b, b_out), (c, c_out)])
+    ]
+    for copy in copies:
+        copy.start()
+    for copy in copies:
+        copy.wait()
 
 
 def on_device(mesh, states, left_ops, right_ops, rows_live, cols_live, block_live):
@@ -293,28 +329,32 @@
     assert nv == 2 and kl % 2 == 0 and ops % 2 == 0
     assert left_ops.shape[1] == 1 and right_ops.shape[1] == 1 and states.shape[1] == 1
     norm = 1.0 / (left_sectors * right_sectors * rows * width)
-    smem = pl.BlockSpec(memory_space=pltpu.SMEM)
-    vmem = pl.BlockSpec(memory_space=pltpu.VMEM)
-    anywhere = pl.BlockSpec(memory_space=pl.ANY)
+    hbm = pl.BlockSpec(memory_space=pltpu.HBM)
     dma = pltpu.SemaphoreType.DMA
     flops = 2 * nv * share * ops * kl * rows * width * (rows + width)
-    return pl.pallas_call(
+    results = pl.pallas_call(
         functools.partial(kernel, n, ops, norm),
         out_shape=(
             jax.ShapeDtypeStruct((nv, share, 1, rows, width), jnp.bfloat16),
             jax.ShapeDtypeStruct((nv, nv), jnp.float32),
             jax.ShapeDtypeStruct((nv, nv), jnp.float32),
         ),
-        in_specs=[smem, smem, smem, anywhere, anywhere, anywhere],
-        out_specs=(vmem, vmem, vmem),
+        in_specs=[hbm] * 6,
+        out_specs=(hbm,) * 3,
         scratch_shapes=[
+            pltpu.VMEM((nv, share, 1, rows, width), jnp.bfloat16),
+            pltpu.VMEM((nv, nv), jnp.float32),
+            pltpu.VMEM((nv, nv), jnp.float32),
+            pltpu.SMEM(rows_live.shape, jnp.int32),
+            pltpu.SMEM(cols_live.shape, jnp.int32),
+            pltpu.SMEM(block_live.shape, jnp.int32),
             pltpu.VMEM((kl, rows, rows), jnp.bfloat16),
             pltpu.VMEM((kl // 2, rows, 2 * rows), jnp.bfloat16),
             pltpu.VMEM((share, ops, kl // 2, rows, 2 * rows), jnp.bfloat16),
             pltpu.VMEM((ops, kl, width, width), jnp.bfloat16),
             pltpu.VMEM((share, nv, rows, width), jnp.bfloat16),
             pltpu.VMEM((n * ops, 8, width), jnp.float32),
-            dma((3,)),
+            dma((9,)),
             dma((n,)),
             dma((share, ops)),
             dma((ops,)),
@@ -325,12 +365,20 @@
             dma,
         ],
         compiler_params=pltpu.CompilerParams(
-            collective_id=0, has_side_effects=True, vmem_limit_bytes=48 * 1024 * 1024
+            collective_id=0, has_side_effects=True, vmem_limit_bytes=63 * 1024 * 1024
         ),
         cost_estimate=pl.CostEstimate(
             flops=flops, bytes_accessed=1 << 20, transcendentals=0
         ),
     )(rows_live, cols_live, block_live, states, left_ops, right_ops)
+    return pl.pallas_call(
+        write_out,
+        out_shape=tuple(jax.ShapeDtypeStruct(r.shape, r.dtype) for r in results),
+        in_specs=[hbm] * 3,
+        out_specs=(hbm,) * 3,
+        scratch_shapes=[dma((3,))],
+        compiler_params=pltpu.CompilerParams(vmem_limit_bytes=63 * 1024 * 1024),
+    )(*results)
 
 
 def solution(mesh):

time: 25.1 us -> 20.7 us (0.82)
  local copies, waits for them, and re-layouts: 6.37 us -> 0 us
  Pallas kernels: 17.8 us -> 19.9 us
    unnamed x15 -> x0, local copies, waits for them, and re-layouts: 6.37 us -> none
    pallas_call x0 -> x1, Pallas kernels: none -> 2.18 us  [on_device(): pl.pallas_call(write_out, out_shape=tuple((jax.ShapeDtypeStruct(r.shape,...]
where the time goes in v2:
time: 20.7 us; the launch traced here: 20.5 us
  Pallas kernels  19.9 us (96%)
  between operations  0.64 us (3%)
    pallas_call x1, Pallas kernels, on_device(): pl.pallas_call(functools.partial(kernel, n, ops, norm), out_shape=(jax.Sh...  17.7 us
    pallas_call x1, Pallas kernels, on_device(): pl.pallas_call(write_out, out_shape=tuple((jax.ShapeDtypeStruct(r.shape,...  2.18 us

profile of v2, /device:TPU:0, one launch (start us, length us, event | category | flops | bytes accessed | tf_op | source)
XLA Modules:
  0.0 20.5 jit_solution(17817678598179198999)
XLA Ops:
  0.6 17.7 %shard_map.85 = (bf16[2,1,1,64,128]{4,3,2,1,0:T(8,128)(2,1)}, f32[2,2]{1,0:T(2,128)}, f32[2,2]{1,0:T(2,128)}) custom-call(s32[4]{0:T(128)} %rows_hbm.1, s32[4]{0:T(128)} %cols_hbm.1, s32[4,4]{1,0:T(4,128)} %blocks_hbm.1, bf16[2,1,4,64,128]{4,3,2,1,0:T(8,128)(2,1)} %states_ref.1, bf16[4,1,64,64]{3,2,1,0:T(8,128)(2,1)} %left_ref.1, ...), custom_call_target="tpu_custom_call" | custom-call | flops 100663296 | bytes 1048576 | tf_op jit(solution)/shard_map/pallas_call | solution.py:335
  18.3 2.2 %shard_map.86 = (bf16[2,1,1,64,128]{4,3,2,1,0:T(8,128)(2,1)}, f32[2,2]{1,0:T(2,128)}, f32[2,2]{1,0:T(2,128)}) custom-call(bf16[2,1,1,64,128]{4,3,2,1,0:T(8,128)(2,1)} %get-tuple-element.6.a, f32[2,2]{1,0:T(2,128)} %get-tuple-element.7.b, f32[2,2]{1,0:T(2,128)} %get-tuple-element.8.c), custom_call_target="tpu_custom_call" | custom-call | tf_op jit(solution)/shard_map/pallas_call | solution.py:374

commit v3 on v2

--- a/solution.py
+++ b/solution.py
@@ -21,10 +21,10 @@
 def kernel(
     n, ops, norm,
     rows_hbm, cols_hbm, blocks_hbm, states_ref, left_ref, right_ref,
-    sigma_out, ray_out, corr_out,
-    sigma_ref, ray_ref, corr_ref,
+    sigma_out, stats,
+    sigma_ref, own_sums,
     rows_ref, cols_ref, blocks_ref,
-    left_own, left_send_buf, left_all, right_all, states_all, stats,
+    left_own, left_send_buf, left_all, right_all, states_all,
     local_sem, left_ss, left_rs, right_ss, right_rs, st_ss, st_rs, stat_ss, stat_rs,
 ):
     s = lax.axis_index("sector")
@@ -36,27 +36,6 @@
     slot = lax.rem(s, share)
     mate = o + 1 - 2 * lax.rem(o, 2)
 
-    load_left = pltpu.make_async_copy(left_ref.at[:, 0], left_own, local_sem.at[0])
-    load_left.start()
-    load_right = pltpu.make_async_copy(right_ref.at[:, 0], right_all.at[o], local_sem.at[1])
-    load_right.start()
-    load_states = pltpu.make_async_copy(
-        states_ref.at[:, 0, s], states_all.at[slot], local_sem.at[2]
-    )
-
-    @pl.when(owner == o)
-    def _():
-        load_states.start()
-
-    tables = [
-        pltpu.make_async_copy(src, dst, local_sem.at[3 + i])
-        for i, (src, dst) in enumerate(
-            [(rows_hbm, rows_ref), (cols_hbm, cols_ref), (blocks_hbm, blocks_ref)]
-        )
-    ]
-    for copy in tables:
-        copy.start()
-
     barrier = pltpu.get_barrier_semaphore()
 
     def greet(r):
@@ -71,6 +50,27 @@
         )
 
     each(n * ops - 1, greet)
+
+    load_left = pltpu.make_async_copy(left_ref.at[:, 0], left_own, local_sem.at[0])
+    load_left.start()
+    load_right = pltpu.make_async_copy(right_ref.at[:, 0], right_all.at[o], local_sem.at[1])
+    load_right.start()
+    load_states = pltpu.make_async_copy(
+        states_ref.at[:, 0, s], states_all.at[slot], local_sem.at[2]
+    )
+
+    @pl.when(owner == o)
+    def _():
+        load_states.start()
+
+    tables = [
+        pltpu.make_async_copy(src, dst, local_sem.at[3 + i])
+        for i, (src, dst) in enumerate(
+            [(rows_hbm, rows_ref), (cols_hbm, cols_ref), (blocks_hbm, blocks_ref)]
+        )
+    ]
+    for copy in tables:
+        copy.start()
 
     load_left.wait()
     packed = [
@@ -249,20 +249,22 @@
             1, share, lambda i, t: tuple(one_block(i, list(t), False)), tuple(totals)
         )
 
+    rank = s * ops + o
     outs = [
-        pltpu.make_async_copy(src, dst, local_sem.at[6 + i])
-        for i, (src, dst) in enumerate(
-            [(sigma_ref, sigma_out), (ray_ref, ray_out), (corr_ref, corr_out)]
-        )
+        pltpu.make_async_copy(sigma_ref, sigma_out, local_sem.at[6]),
+        pltpu.make_async_copy(own_sums, stats.at[rank], local_sem.at[7]),
     ]
-    outs[0].start()
-
-    rank = s * ops + o
-    stats[rank] = jnp.concatenate(list(totals), axis=0)
+
+    sums = jnp.sum(jnp.concatenate(list(totals), axis=0), axis=1, keepdims=True)
+    at_row = lax.broadcasted_iota(jnp.int32, (8, width), 0)
+    at_lane = lax.broadcasted_iota(jnp.int32, (8, width), 1)
+    own_sums[...] = jnp.sum(
+        jnp.where(at_row == at_lane, sums * norm, 0.0), axis=0, keepdims=True
+    )
 
     def tell(r):
         pltpu.make_async_remote_copy(
-            src_ref=stats.at[rank],
+            src_ref=own_sums,
             dst_ref=stats.at[rank],
             send_sem=stat_ss,
             recv_sem=stat_rs,
@@ -274,6 +276,8 @@
         ).start()
 
     each(n * ops - 1, tell)
+    for copy in outs:
+        copy.start()
 
     for copy in sends:
         copy.wait_send()
@@ -295,25 +299,30 @@
     )
     both.wait_recv()
     both.wait_send()
-    result = jnp.sum(jnp.sum(stats[...], axis=0), axis=1, keepdims=True) * norm
-    for v in range(2):
-        for w in range(2):
-            at = 2 * v + w
-            ray_ref[v:v + 1, w:w + 1] = result[at:at + 1]
-            corr_ref[v:v + 1, w:w + 1] = result[4 + at:5 + at]
-    for copy in outs[1:]:
-        copy.start()
     for copy in outs:
         copy.wait()
 
 
-def write_out(a, b, c, a_out, b_out, c_out, sem):
+def write_out(
+    sigma_in, stats_in, sigma_out, ray_out, corr_out, sigma, stats, ray, corr, in_sem, out_sem
+):
+    load_sigma = pltpu.make_async_copy(sigma_in, sigma, in_sem.at[0])
+    load_stats = pltpu.make_async_copy(stats_in, stats, in_sem.at[1])
+    load_stats.start()
+    load_sigma.start()
+    load_stats.wait()
+    result = jnp.sum(stats[...], axis=0)
+    for v in range(2):
+        ray[v:v + 1, :] = result[:, 2 * v:2 * v + 2]
+        corr[v:v + 1, :] = result[:, 4 + 2 * v:6 + 2 * v]
     copies = [
-        pltpu.make_async_copy(src, dst, sem.at[i])
-        for i, (src, dst) in enumerate([(a, a_out), (b, b_out), (c, c_out)])
+        pltpu.make_async_copy(src, dst, out_sem.at[i])
+        for i, (src, dst) in enumerate([(ray, ray_out), (corr, corr_out), (sigma, sigma_out)])
     ]
-    for copy in copies:
-        copy.start()
+    copies[0].start()
+    copies[1].start()
+    load_sigma.wait()
+    copies[2].start()
     for copy in copies:
         copy.wait()
 
@@ -332,19 +341,17 @@
     hbm = pl.BlockSpec(memory_space=pltpu.HBM)
     dma = pltpu.SemaphoreType.DMA
     flops = 2 * nv * share * ops * kl * rows * width * (rows + width)
-    results = pl.pallas_call(
+    sigma, stats = pl.pallas_call(
         functools.partial(kernel, n, ops, norm),
         out_shape=(
             jax.ShapeDtypeStruct((nv, share, 1, rows, width), jnp.bfloat16),
-            jax.ShapeDtypeStruct((nv, nv), jnp.float32),
-            jax.ShapeDtypeStruct((nv, nv), jnp.float32),
+            jax.ShapeDtypeStruct((n * ops, 1, width), jnp.float32),
         ),
         in_specs=[hbm] * 6,
-        out_specs=(hbm,) * 3,
+        out_specs=(hbm,) * 2,
         scratch_shapes=[
             pltpu.VMEM((nv, share, 1, rows, width), jnp.bfloat16),
-            pltpu.VMEM((nv, nv), jnp.float32),
-            pltpu.VMEM((nv, nv), jnp.float32),
+            pltpu.VMEM((1, width), jnp.float32),
             pltpu.SMEM(rows_live.shape, jnp.int32),
             pltpu.SMEM(cols_live.shape, jnp.int32),
             pltpu.SMEM(block_live.shape, jnp.int32),
@@ -353,8 +360,7 @@
             pltpu.VMEM((share, ops, kl // 2, rows, 2 * rows), jnp.bfloat16),
             pltpu.VMEM((ops, kl, width, width), jnp.bfloat16),
             pltpu.VMEM((share, nv, rows, width), jnp.bfloat16),
-            pltpu.VMEM((n * ops, 8, width), jnp.float32),
-            dma((9,)),
+            dma((8,)),
             dma((n,)),
             dma((share, ops)),
             dma((ops,)),
@@ -373,12 +379,23 @@
     )(rows_live, cols_live, block_live, states, left_ops, right_ops)
     return pl.pallas_call(
         write_out,
-        out_shape=tuple(jax.ShapeDtypeStruct(r.shape, r.dtype) for r in results),
-        in_specs=[hbm] * 3,
+        out_shape=(
+            jax.ShapeDtypeStruct(sigma.shape, sigma.dtype),
+            jax.ShapeDtypeStruct((nv, nv), jnp.float32),
+            jax.ShapeDtypeStruct((nv, nv), jnp.float32),
+        ),
+        in_specs=[hbm] * 2,
         out_specs=(hbm,) * 3,
-        scratch_shapes=[dma((3,))],
+        scratch_shapes=[
+            pltpu.VMEM(sigma.shape, sigma.dtype),
+            pltpu.VMEM(stats.shape, stats.dtype),
+            pltpu.VMEM((nv, nv), jnp.float32),
+            pltpu.VMEM((nv, nv), jnp.float32),
+            dma((2,)),
+            dma((3,)),
+        ],
         compiler_params=pltpu.CompilerParams(vmem_limit_bytes=63 * 1024 * 1024),
-    )(*results)
+    )(sigma, stats)
 
 
 def solution(mesh):

time: 20.7 us -> 19.2 us (0.928)
  Pallas kernels: 19.9 us -> 18.4 us
    pallas_call x1, Pallas kernels: 17.7 us -> 16.9 us  [on_device(): pl.pallas_call(functools.partial(kernel, n, ops, norm), out_shape=(jax.Sh...]
    pallas_call x1, Pallas kernels: 2.18 us -> 1.45 us  [on_device(): pl.pallas_call(write_out, out_shape=(jax.ShapeDtypeStruct(sigma.shape, si...]
where the time goes in v3:
time: 19.2 us; the launch traced here: 19 us
  Pallas kernels  18.4 us (96%)
  between operations  0.64 us (3%)
    pallas_call x1, Pallas kernels, on_device(): pl.pallas_call(functools.partial(kernel, n, ops, norm), out_shape=(jax.Sh...  16.9 us
    pallas_call x1, Pallas kernels, on_device(): pl.pallas_call(write_out, out_shape=(jax.ShapeDtypeStruct(sigma.shape, si...  1.45 us

profile of v3, /device:TPU:0, one launch (start us, length us, event | category | flops | bytes accessed | tf_op | source)
XLA Modules:
  0.0 19.0 jit_solution(11158672946213295690)
XLA Ops:
  0.6 16.9 %shard_map.85 = (bf16[2,1,1,64,128]{4,3,2,1,0:T(8,128)(2,1)}, f32[16,1,128]{2,1,0:T(1,128)}) custom-call(s32[4]{0:T(128)} %rows_hbm.1, s32[4]{0:T(128)} %cols_hbm.1, s32[4,4]{1,0:T(4,128)} %blocks_hbm.1, bf16[2,1,4,64,128]{4,3,2,1,0:T(8,128)(2,1)} %states_ref.1, bf16[4,1,64,64]{3,2,1,0:T(8,128)(2,1)} %left_ref.1, bf16[4,1,128,128]{3,2,1,0:T(8,128)(2,1)} %right_ref.1), custom_call_target="tpu_custom_call" | custom-call | flops 100663296 | bytes 1048576 | tf_op jit(solution)/shard_map/pallas_call | solution.py:344
  17.6 1.4 %shard_map.86 = (bf16[2,1,1,64,128]{4,3,2,1,0:T(8,128)(2,1)}, f32[2,2]{1,0:T(2,128)}, f32[2,2]{1,0:T(2,128)}) custom-call(bf16[2,1,1,64,128]{4,3,2,1,0:T(8,128)(2,1)} %get-tuple-element.5.sigma_in, f32[16,1,128]{2,1,0:T(1,128)} %get-tuple-element.6.stats_in), custom_call_target="tpu_custom_call" | custom-call | tf_op jit(solution)/shard_map/pallas_call | solution.py:380

commit v4 on v3

--- a/solution.py
+++ b/solution.py
@@ -178,6 +178,15 @@
             )
             for m in narrow
         ]
+
+        def products(right):
+            return [
+                jnp.sum(masked[v] * right[w], axis=0, keepdims=True)
+                for v in range(2)
+                for w in range(2)
+            ]
+
+        overlaps = products(masked)
         acc = jnp.zeros((2 * rows, width), jnp.float32)
         for step in range(ops):
             if step == 0:
@@ -216,11 +225,7 @@
         ]
         for v in range(2):
             sigma_ref[v, i, 0] = summed[v].astype(jnp.bfloat16)
-        out = []
-        for right in (summed, masked):
-            for v in range(2):
-                for w in range(2):
-                    out.append(jnp.sum(masked[v] * right[w], axis=0, keepdims=True))
+        out = products(summed) + overlaps
         return [x + y for x, y in zip(totals, out)]
 
     def state_copy_in(i):

time: 19.2 us -> 19.2 us (level)
  no operation moved by 1% of the time
where the time goes in v4:
time: 19.2 us; the launch traced here: 19 us
  Pallas kernels  18.4 us (96%)
  between operations  0.64 us (3%)
    pallas_call x1, Pallas kernels, on_device(): pl.pallas_call(functools.partial(kernel, n, ops, norm), out_shape=(jax.Sh...  16.9 us
    pallas_call x1, Pallas kernels, on_device(): pl.pallas_call(write_out, out_shape=(jax.ShapeDtypeStruct(sigma.shape, si...  1.45 us

profile of v4, /device:TPU:0, one launch (start us, length us, event | category | flops | bytes accessed | tf_op | source)
XLA Modules:
  0.0 19.0 jit_solution(2377899743508133941)
XLA Ops:
  0.6 16.9 %shard_map.85 = (bf16[2,1,1,64,128]{4,3,2,1,0:T(8,128)(2,1)}, f32[16,1,128]{2,1,0:T(1,128)}) custom-call(s32[4]{0:T(128)} %rows_hbm.1, s32[4]{0:T(128)} %cols_hbm.1, s32[4,4]{1,0:T(4,128)} %blocks_hbm.1, bf16[2,1,4,64,128]{4,3,2,1,0:T(8,128)(2,1)} %states_ref.1, bf16[4,1,64,64]{3,2,1,0:T(8,128)(2,1)} %left_ref.1, bf16[4,1,128,128]{3,2,1,0:T(8,128)(2,1)} %right_ref.1), custom_call_target="tpu_custom_call" | custom-call | flops 100663296 | bytes 1048576 | tf_op jit(solution)/shard_map/pallas_call | solution.py:349
  17.6 1.4 %shard_map.86 = (bf16[2,1,1,64,128]{4,3,2,1,0:T(8,128)(2,1)}, f32[2,2]{1,0:T(2,128)}, f32[2,2]{1,0:T(2,128)}) custom-call(bf16[2,1,1,64,128]{4,3,2,1,0:T(8,128)(2,1)} %get-tuple-element.5.sigma_in, f32[16,1,128]{2,1,0:T(1,128)} %get-tuple-element.6.stats_in), custom_call_target="tpu_custom_call" | custom-call | tf_op jit(solution)/shard_map/pallas_call | solution.py:385

commit v5 on v3

--- a/solution.py
+++ b/solution.py
@@ -49,7 +49,7 @@
             device_id_type=MESH,
         )
 
-    each(n * ops - 1, greet)
+    each(n * ops - 1, lambda r: greet(n * ops - 2 - r))
 
     load_left = pltpu.make_async_copy(left_ref.at[:, 0], left_own, local_sem.at[0])
     load_left.start()
@@ -275,7 +275,7 @@
             device_id_type=MESH,
         ).start()
 
-    each(n * ops - 1, tell)
+    each(n * ops - 1, lambda r: tell(n * ops - 2 - r))
     for copy in outs:
         copy.start()
 

time: 19.2 us -> 19.3 us (level)
  no operation moved by 1% of the time
where the time goes in v5:
time: 19.3 us; the launch traced here: 19.1 us
  Pallas kernels  18.4 us (95%)
  between operations  0.64 us (3%)
    pallas_call x1, Pallas kernels, on_device(): pl.pallas_call(functools.partial(kernel, n, ops, norm), out_shape=(jax.Sh...  17 us
    pallas_call x1, Pallas kernels, on_device(): pl.pallas_call(write_out, out_shape=(jax.ShapeDtypeStruct(sigma.shape, si...  1.45 us

profile of v5, /device:TPU:0, one launch (start us, length us, event | category | flops | bytes accessed | tf_op | source)
XLA Modules:
  0.0 19.1 jit_solution(5084636520878674687)
XLA Ops:
  0.6 17.0 %shard_map.85 = (bf16[2,1,1,64,128]{4,3,2,1,0:T(8,128)(2,1)}, f32[16,1,128]{2,1,0:T(1,128)}) custom-call(s32[4]{0:T(128)} %rows_hbm.1, s32[4]{0:T(128)} %cols_hbm.1, s32[4,4]{1,0:T(4,128)} %blocks_hbm.1, bf16[2,1,4,64,128]{4,3,2,1,0:T(8,128)(2,1)} %states_ref.1, bf16[4,1,64,64]{3,2,1,0:T(8,128)(2,1)} %left_ref.1, bf16[4,1,128,128]{3,2,1,0:T(8,128)(2,1)} %right_ref.1), custom_call_target="tpu_custom_call" | custom-call | flops 100663296 | bytes 1048576 | tf_op jit(solution)/shard_map/pallas_call | solution.py:344
  17.6 1.4 %shard_map.86 = (bf16[2,1,1,64,128]{4,3,2,1,0:T(8,128)(2,1)}, f32[2,2]{1,0:T(2,128)}, f32[2,2]{1,0:T(2,128)}) custom-call(bf16[2,1,1,64,128]{4,3,2,1,0:T(8,128)(2,1)} %get-tuple-element.5.sigma_in, f32[16,1,128]{2,1,0:T(1,128)} %get-tuple-element.6.stats_in), custom_call_target="tpu_custom_call" | custom-call | tf_op jit(solution)/shard_map/pallas_call | solution.py:380
